TPU v7x, 32 devices: a whole 2x2x4 slice. The times are simulated.
32 devices in a mesh: group: 2 (over x), row: 16 (over z, y, core).
Axes of the slice: x: 2, y: 2, z: 4, core: 2. Of those that a mesh axis runs over, the one named last changes fastest.
Arguments:
- near_tiles: bfloat16 [2, 5, 1024, 1024], replicated, may hold values from -0.1875 to 0.1875
- near_order: int32 [5], replicated, may hold values from 0 to 4, each once
- receiver_basis: bfloat16 [2, 1024, 16], replicated, may hold values from -1.5 to 1.5
- source_basis: bfloat16 [2, 1024, 16], replicated, may hold values from -0.1875 to 0.1875
- coupling: float32 [2, 16, 16, 16], replicated, may hold values from -0.375 to 0.375
- initial_model: bfloat16 [2, 128, 16384], P(None, 'group', 'row'), parts along dimension 1, may hold values from -6 to 6
- observed: bfloat16 [128, 16384], P('group', 'row'), parts along dimension 0, may hold values from -18 to 18
Outputs:
- model_out: float32 [2, 128, 16384], P(None, 'group', 'row'), parts along dimension 1
- misfit: float32 [128, 16384], P('group', 'row'), parts along dimension 0
There are 2 independent parts, one for each index of `group`. A program takes and returns all parts, laid end to end along the dimension named above; an argument that names none is the same for every part. Nothing has to cross between parts.
Inputs may be any that keep to these rules, and one draw needn't show every extreme that they name: `near_order`: a permutation of 0 to 4.
All inputs are finite; a program needn't handle non-finite values.
Results may differ from a plain program's by a relative error of at most 0.0029.
Values may be sent and summed in bfloat16 or wider, within the bound.
A program may use at most 128 MiB of HBM per device.

v0:
```python
import jax
import jax.numpy as jnp
from jax import lax
from jax.sharding import PartitionSpec as P

RADIUS = 2
ITERS = 3


def shifted(block, axis, distance):
    devices = range(lax.axis_size(axis))
    route = [((i - distance) % len(devices), i) for i in devices]
    return lax.ppermute(block, axis, route)


def on_device(
    near_tiles, near_order, receiver_basis, source_basis, coupling, initial_model, observed
):
    highest = lax.Precision.HIGHEST
    band_count = coupling.shape[1]
    own_band = lax.axis_index("row")
    inverse = jnp.argsort(near_order)
    tile_list = [
        lax.dynamic_index_in_dim(near_tiles, inverse[offset_slot], 1, keepdims=False)
        for offset_slot in range(2 * RADIUS + 1)
    ]
    receiver_full = receiver_basis.astype(jnp.float32)
    source_full = source_basis.astype(jnp.float32)
    model = initial_model.astype(jnp.float32)
    measured = observed.astype(jnp.float32)
    layer_count, pert_count, point_count = model.shape
    misfit = measured
    for step_index in range(ITERS):
        model_wire = model.astype(jnp.bfloat16)
        received_map = {0: model_wire}
        for heading in (1, -1):
            current = model_wire
            for distance in range(1, RADIUS + 1):
                current = shifted(current, "row", heading)
                received_map[heading * distance] = current
        predicted = jnp.zeros((pert_count, point_count), jnp.float32)
        for offset_slot in range(2 * RADIUS + 1):
            shift_by = offset_slot - RADIUS
            predicted = predicted + jnp.einsum(
                "lpc,lac->pa",
                received_map[shift_by],
                tile_list[offset_slot],
                preferred_element_type=jnp.float32,
            )
        summary = jnp.einsum(
            "lpc,lcs->lsp", model_wire, source_basis, preferred_element_type=jnp.float32
        )
        add_received = lax.all_gather(summary[None], "row", axis=0, tiled=True)
        sources = jnp.arange(add_received.shape[0], dtype=jnp.int32)
        chosen = jnp.take(coupling, (own_band - sources) % band_count, axis=1)
        far_field = jnp.einsum("ljrs,jlsp->lrp", chosen, add_received, precision=highest)
        predicted = predicted + jnp.einsum(
            "lar,lrp->pa", receiver_full, far_field, precision=highest
        )
        misfit = measured - predicted
        misfit_wire = misfit.astype(jnp.bfloat16)
        gradient = jnp.zeros_like(model)
        for offset_slot in range(2 * RADIUS + 1):
            shift_by = offset_slot - RADIUS
            if shift_by == 0:
                received = misfit_wire
            else:
                received = shifted(misfit_wire, "row", -shift_by)
            gradient = gradient + jnp.einsum(
                "pa,lac->lpc", received, tile_list[offset_slot], preferred_element_type=jnp.float32
            )
        data_summary = jnp.einsum(
            "lar,pa->lrp", receiver_full, misfit_wire.astype(jnp.float32), precision=highest
        )

        def add_back(received):
            sources = jnp.arange(received.shape[0], dtype=jnp.int32)
            chosen = jnp.take(coupling, (sources - own_band) % band_count, axis=1)
            return jnp.einsum("lirs,ilrp->lsp", chosen, received, precision=highest)

        far_back = add_back(lax.all_gather(data_summary[None], "row", axis=0, tiled=True))
        gradient = gradient + jnp.einsum("lcs,lsp->lpc", source_full, far_back, precision=highest)
        model = model + 0.01 * (gradient - 10.0 * model)
    return (model, misfit)


def solution(mesh):
    placed = (P(), P(), P(), P(), P(), P(None, "group", "row"), P("group", "row"))
    return jax.shard_map(
        on_device,
        mesh=mesh,
        in_specs=placed,
        out_specs=(P(None, "group", "row"), P("group", "row")),
        check_vma=False,
    )
```

profile of v0, /device:TPU:0, one launch (start us, length us, event | category | flops | bytes accessed | tf_op | source)
XLA Modules:
  0.0 225.3 jit_solution(1642247805543370166)
XLA Ops:
  0.7 5.5 %collective-permute-start = (bf16[2,64,1024]{2,1,0:T(8,128)(2,1)}, bf16[2,64,1024]{2,1,0:T(8,128)(2,1)S(1)}, u32[]{:S(2)}, u32[]{:S(2)}) collective-permute-start(bf16[2,64,1024]{2,1,0:T(8,128)(2,1)} %param.14), channel_id=1, source_target_pairs={{1,0},{2,1},{3,2},{4,3},{5,4},{6,5},{7,6},{8,7},{9,8},{10,9},{11,1... | collective-permute-start | bytes 786440 | tf_op jit(solution)/shard_map/ppermute | solution.py:13
  6.2 1.6 sort.17
  11.0 18.9 %all-gather = f32[32,16,64]{2,1,0:T(8,128)S(1)} all-gather(f32[2,16,64]{2,1,0:T(8,128)S(1)} %fusion.360), channel_id=2, replica_groups=mesh['group'=2,'row'=16] {'row'}, dimensions={0}, use_global_device_ids=true | all-gather | bytes 139264 | tf_op jit(solution)/shard_map/all_gather | solution.py:53
  31.2 3.6 %fusion.189 = f32[1024,64]{0,1:T(8,128)S(1)} fusion(bf16[2,64,1024]{2,1,0:T(8,128)(2,1)} %param.14, bf16[2,5,1024,1024]{3,2,1,0:T(8,128)(2,1)} %param.9, s32[]{:T(128)S(6)} %select_n.44), kind=kOutput, calls=%fused_computation.125 | convolution fusion | flops 268435456 | bytes 4718596 | tf_op jit(solution)/shard_map/lpc,lac->pa/dot_general | solution.py:44
  46.5 3.7 %fusion.180 = f32[1024,64]{0,1:T(8,128)S(1)} fusion(bf16[2,64,1024]{2,1,0:T(8,128)(2,1)S(1)} %collective-permute-done, bf16[2,5,1024,1024]{3,2,1,0:T(8,128)(2,1)} %param.9, s32[]{:T(128)S(6)} %select_n.43), kind=kOutput, calls=%fused_computation.122 | convolution fusion | flops 268435456 | bytes 4718596 | tf_op jit(solution)/shard_map/lpc,lac->pa/dot_general | solution.py:44
  50.3 4.3 %fusion.270 = f32[1024,64]{0,1:T(8,128)S(1)} fusion(f32[1024,64]{0,1:T(8,128)S(1)} %fusion.189, f32[1024,64]{0,1:T(8,128)S(1)} %fusion.180, bf16[2,64,1024]{2,1,0:T(8,128)(2,1)S(1)} %collective-permute-done.1, bf16[2,5,1024,1024]{3,2,1,0:T(8,128)(2,1)} %param.9, s32[]{:T(128)S(6)} %select_n.42), kind=kOutput, calls=%fused_computation.155 | convolution fusion | flops 268566528 | bytes 5242884 | tf_op jit(solution)/shard_map/lpc,lac->pa/dot_general | solution.py:44
  54.6 3.9 %fusion.252 = f32[1024,64]{0,1:T(8,128)S(1)} fusion(f32[1024,64]{0,1:T(8,128)S(1)} %fusion.270, bf16[2,64,1024]{2,1,0:T(8,128)(2,1)S(1)} %collective-permute-done.2, bf16[2,5,1024,1024]{3,2,1,0:T(8,128)(2,1)} %param.9, s32[]{:T(128)S(6)} %select_n.45), kind=kOutput, calls=%fused_computation.149 | convolution fusion | flops 268500992 | bytes 4980740 | tf_op jit(solution)/shard_map/lpc,lac->pa/dot_general | solution.py:44
  58.5 3.6 %fusion.273 = bf16[64,1024]{1,0:T(8,128)(2,1)S(1)} fusion(f32[64,1024]{1,0:T(8,128)S(1)} %convolution_bitcast_fusion.2, f32[1024,64]{0,1:T(8,128)S(1)} %fusion.252, bf16[2,64,1024]{2,1,0:T(8,128)(2,1)S(1)} %collective-permute-done.3, bf16[2,5,1024,1024]{3,2,1,0:T(8,128)(2,1)} %param.9, s32[]{:T(128)S(6)} %select_n.46, bf16[64,1024]{1,0:T(8,128)(2,1)S(1)} %copy-done.5), kind=kOutput, calls=%fused_computation.156 | convolution fusion | flops 268763136 | bytes 5242884 | tf_op jit(solution)/shard_map/lpc,lac->pa/dot_general | solution.py:44
  62.5 3.7 %collective-permute-start.6 = (bf16[64,1024]{1,0:T(8,128)(2,1)S(1)}, bf16[64,1024]{1,0:T(8,128)(2,1)S(1)}, u32[]{:S(2)}, u32[]{:S(2)}) collective-permute-start(bf16[64,1024]{1,0:T(8,128)(2,1)S(1)} %fusion.273), channel_id=1, source_target_pairs={{1,0},{2,1},{3,2},{4,3},{5,4},{6,5},{7,6},{8,7},{9,8},{10,9},{11,1... | collective-permute-start | bytes 393224 | tf_op jit(solution)/shard_map/ppermute | solution.py:13
  66.3 1.7 collective-permute-start.4
  69.0 21.0 %all-gather.1 = f32[32,16,64]{2,1,0:T(8,128)S(1)} all-gather(f32[2,16,64]{2,1,0:T(8,128)S(1)} %bitcast.475), channel_id=3, replica_groups=mesh['group'=2,'row'=16] {'row'}, dimensions={0}, use_global_device_ids=true | all-gather | bytes 139264 | tf_op jit(solution)/shard_map/all_gather | solution.py:81
  95.1 1.4 fusion.192
  97.0 19.6 %all-gather.2 = f32[32,16,64]{2,1,0:T(8,128)S(1)} all-gather(f32[2,16,64]{2,1,0:T(8,128)S(1)} %convolution_bitcast_fusion.4), channel_id=4, replica_groups=mesh['group'=2,'row'=16] {'row'}, dimensions={0}, use_global_device_ids=true | all-gather | bytes 139264 | tf_op jit(solution)/shard_map/all_gather | solution.py:53
  119.7 2.0 collective-permute-done.9
  121.7 1.4 fusion.264
  123.1 1.4 fusion.249
  124.5 2.2 collective-permute-done.11
  126.7 1.4 fusion.276
  129.0 1.8 collective-permute-start.14
  130.8 1.7 collective-permute-start.12
  133.3 21.1 %all-gather.3 = f32[32,16,64]{2,1,0:T(8,128)S(1)} all-gather(f32[2,16,64]{2,1,0:T(8,128)S(1)} %bitcast.474), channel_id=5, replica_groups=mesh['group'=2,'row'=16] {'row'}, dimensions={0}, use_global_device_ids=true | all-gather | bytes 139264 | tf_op jit(solution)/shard_map/all_gather | solution.py:81
  159.4 1.4 fusion.195
  161.3 19.7 %all-gather.4 = f32[32,16,64]{2,1,0:T(8,128)S(1)} all-gather(f32[2,16,64]{2,1,0:T(8,128)S(1)} %convolution_bitcast_fusion.3), channel_id=6, replica_groups=mesh['group'=2,'row'=16] {'row'}, dimensions={0}, use_global_device_ids=true | all-gather | bytes 139264 | tf_op jit(solution)/shard_map/all_gather | solution.py:53
  182.9 1.4 fusion.186
  184.3 2.1 collective-permute-done.17
  187.8 1.4 fusion.246
  189.2 2.2 collective-permute-done.19
  191.4 2.1 fusion.359
  194.3 1.8 collective-permute-start.22
  196.2 1.7 collective-permute-start.20
  198.7 21.1 %all-gather.5 = f32[32,16,64]{2,1,0:T(8,128)S(1)} all-gather(f32[2,16,64]{2,1,0:T(8,128)S(1)} %bitcast.473), channel_id=7, replica_groups=mesh['group'=2,'row'=16] {'row'}, dimensions={0}, use_global_device_ids=true | all-gather | bytes 139264 | tf_op jit(solution)/shard_map/all_gather | solution.py:81
  223.5 1.9 fusion.168
  (92 shorter events, 32.1 us)
Async XLA Ops:
  0.6 30.0 %copy-start = (f32[2,16,16,16]{3,2,1,0:T(8,128)S(1)}, f32[2,16,16,16]{3,2,1,0:T(8,128)}, u32[]{:S(2)}) copy-start(f32[2,16,16,16]{3,2,1,0:T(8,128)} %param.13) | copy-start | bytes 98308
  0.6 90.0 %copy-start.3 = (bf16[2,1024,16]{1,2,0:T(8,128)(2,1)S(1)}, bf16[2,1024,16]{1,2,0:T(8,128)(2,1)}, u32[]{:S(2)}) copy-start(bf16[2,1024,16]{1,2,0:T(8,128)(2,1)} %param.12) | copy-start | bytes 196612
  0.7 68.2 %copy-start.4 = (bf16[2,1024,16]{1,2,0:T(8,128)(2,1)S(1)}, bf16[2,1024,16]{1,2,0:T(8,128)(2,1)}, u32[]{:S(2)}) copy-start(bf16[2,1024,16]{1,2,0:T(8,128)(2,1)} %param.11) | copy-start | bytes 196612
  0.7 57.8 %copy-start.5 = (bf16[64,1024]{1,0:T(8,128)(2,1)S(1)}, bf16[64,1024]{1,0:T(8,128)(2,1)}, u32[]{:S(2)}) copy-start(bf16[64,1024]{1,0:T(8,128)(2,1)} %param.15) | copy-start | bytes 393220
  0.7 36.1 %collective-permute-start = (bf16[2,64,1024]{2,1,0:T(8,128)(2,1)}, bf16[2,64,1024]{2,1,0:T(8,128)(2,1)S(1)}, u32[]{:S(2)}, u32[]{:S(2)}) collective-permute-start(bf16[2,64,1024]{2,1,0:T(8,128)(2,1)} %param.14), channel_id=1, source_target_pairs={{1,0},{2,1},{3,2},{4,3},{5,4},{6,5},{7,6},{8,7},{9,8},{10,9},{11,1... | collective-permute-start | bytes 786440 | tf_op jit(solution)/shard_map/ppermute | solution.py:13
  6.2 40.3 %collective-permute-start.2 = (bf16[2,64,1024]{2,1,0:T(8,128)(2,1)}, bf16[2,64,1024]{2,1,0:T(8,128)(2,1)S(1)}, u32[]{:S(2)}, u32[]{:S(2)}) collective-permute-start(bf16[2,64,1024]{2,1,0:T(8,128)(2,1)} %param.14), channel_id=1, source_target_pairs={{15,0},{0,1},{1,2},{2,3},{3,4},{4,5},{5,6},{6,7},{7,8},{8,9},{9,10... | collective-permute-start | bytes 786440 | tf_op jit(solution)/shard_map/ppermute | solution.py:13
  36.8 13.5 %collective-permute-start.1 = (bf16[2,64,1024]{2,1,0:T(8,128)(2,1)S(1)}, bf16[2,64,1024]{2,1,0:T(8,128)(2,1)S(1)}, u32[]{:S(2)}, u32[]{:S(2)}) collective-permute-start(bf16[2,64,1024]{2,1,0:T(8,128)(2,1)S(1)} %collective-permute-done), channel_id=1, source_target_pairs={{1,0},{2,1},{3,2},{4,3},{5,4},{6,5},{7,6},{8,7},{9,8},{10,9},{11,1... | collective-permute-start | bytes 786440 | tf_op jit(solution)/shard_map/ppermute | solution.py:13
  46.4 21.6 %copy-start.1 = (bf16[2,5,1024,1024]{3,2,1,0:T(8,128)(2,1)S(1)}, bf16[2,5,1024,1024]{3,2,1,0:T(8,128)(2,1)}, u32[]{:S(2)}) copy-start(bf16[2,5,1024,1024]{3,2,1,0:T(8,128)(2,1)} %param.9) | copy-start | bytes 62914564
  46.4 12.1 %collective-permute-start.3 = (bf16[2,64,1024]{2,1,0:T(8,128)(2,1)S(1)}, bf16[2,64,1024]{2,1,0:T(8,128)(2,1)S(1)}, u32[]{:S(2)}, u32[]{:S(2)}) collective-permute-start(bf16[2,64,1024]{2,1,0:T(8,128)(2,1)S(1)} %collective-permute-done.2), channel_id=1, source_target_pairs={{15,0},{0,1},{1,2},{2,3},{3,4},{4,5},{5,6},{6,7},{7,8},{8,9},{9,10... | collective-permute-start | bytes 786440 | tf_op jit(solution)/shard_map/ppermute | solution.py:13
  50.2 43.4 %copy-start.2 = (bf16[2,64,1024]{2,1,0:T(8,128)(2,1)S(1)}, bf16[2,64,1024]{2,1,0:T(8,128)(2,1)}, u32[]{:S(2)}) copy-start(bf16[2,64,1024]{2,1,0:T(8,128)(2,1)} %param.14) | copy-start | bytes 786436
  62.1 30.6 %collective-permute-start.7 = (bf16[64,1024]{1,0:T(8,128)(2,1)S(1)}, bf16[64,1024]{1,0:T(8,128)(2,1)S(1)}, u32[]{:S(2)}, u32[]{:S(2)}) collective-permute-start(bf16[64,1024]{1,0:T(8,128)(2,1)S(1)} %fusion.273), channel_id=1, source_target_pairs={{2,0},{3,1},{4,2},{5,3},{6,4},{7,5},{8,6},{9,7},{10,8},{11,9},{12,... | collective-permute-start | bytes 393224 | tf_op jit(solution)/shard_map/ppermute | solution.py:13
  62.5 29.4 %collective-permute-start.6 = (bf16[64,1024]{1,0:T(8,128)(2,1)S(1)}, bf16[64,1024]{1,0:T(8,128)(2,1)S(1)}, u32[]{:S(2)}, u32[]{:S(2)}) collective-permute-start(bf16[64,1024]{1,0:T(8,128)(2,1)S(1)} %fusion.273), channel_id=1, source_target_pairs={{1,0},{2,1},{3,2},{4,3},{5,4},{6,5},{7,6},{8,7},{9,8},{10,9},{11,1... | collective-permute-start | bytes 393224 | tf_op jit(solution)/shard_map/ppermute | solution.py:13
  66.3 24.8 %collective-permute-start.5 = (bf16[64,1024]{1,0:T(8,128)(2,1)S(1)}, bf16[64,1024]{1,0:T(8,128)(2,1)S(1)}, u32[]{:S(2)}, u32[]{:S(2)}) collective-permute-start(bf16[64,1024]{1,0:T(8,128)(2,1)S(1)} %fusion.273), channel_id=1, source_target_pairs={{15,0},{0,1},{1,2},{2,3},{3,4},{4,5},{5,6},{6,7},{7,8},{8,9},{9,10... | collective-permute-start | bytes 393224 | tf_op jit(solution)/shard_map/ppermute | solution.py:13
  66.3 27.3 %collective-permute-start.4 = (bf16[64,1024]{1,0:T(8,128)(2,1)S(1)}, bf16[64,1024]{1,0:T(8,128)(2,1)S(1)}, u32[]{:S(2)}, u32[]{:S(2)}) collective-permute-start(bf16[64,1024]{1,0:T(8,128)(2,1)S(1)} %fusion.273), channel_id=1, source_target_pairs={{14,0},{15,1},{0,2},{1,3},{2,4},{3,5},{4,6},{5,7},{6,8},{7,9},{8,1... | collective-permute-start | bytes 393224 | tf_op jit(solution)/shard_map/ppermute | solution.py:13
  94.9 22.5 %collective-permute-start.8 = (bf16[2,64,1024]{2,1,0:T(8,128)(2,1)S(1)}, bf16[2,64,1024]{2,1,0:T(8,128)(2,1)S(1)}, u32[]{:S(2)}, u32[]{:S(2)}) collective-permute-start(bf16[2,64,1024]{2,1,0:T(8,128)(2,1)S(1)} %get-tuple-element.10), channel_id=1, source_target_pairs={{1,0},{2,1},{3,2},{4,3},{5,4},{6,5},{7,6},{8,7},{9,8},{10,9},{11,1... | collective-permute-start | bytes 786440 | tf_op jit(solution)/shard_map/ppermute | solution.py:13
  96.5 21.7 %collective-permute-start.10 = (bf16[2,64,1024]{2,1,0:T(8,128)(2,1)S(1)}, bf16[2,64,1024]{2,1,0:T(8,128)(2,1)S(1)}, u32[]{:S(2)}, u32[]{:S(2)}) collective-permute-start(bf16[2,64,1024]{2,1,0:T(8,128)(2,1)S(1)} %get-tuple-element.10), channel_id=1, source_target_pairs={{15,0},{0,1},{1,2},{2,3},{3,4},{4,5},{5,6},{6,7},{7,8},{8,9},{9,10... | collective-permute-start | bytes 786440 | tf_op jit(solution)/shard_map/ppermute | solution.py:13
  117.4 4.3 %collective-permute-start.9 = (bf16[2,64,1024]{2,1,0:T(8,128)(2,1)S(1)}, bf16[2,64,1024]{2,1,0:T(8,128)(2,1)S(1)}, u32[]{:S(2)}, u32[]{:S(2)}) collective-permute-start(bf16[2,64,1024]{2,1,0:T(8,128)(2,1)S(1)} %collective-permute-done.8), channel_id=1, source_target_pairs={{1,0},{2,1},{3,2},{4,3},{5,4},{6,5},{7,6},{8,7},{9,8},{10,9},{11,1... | collective-permute-start | bytes 786440 | tf_op jit(solution)/shard_map/ppermute | solution.py:13
  118.1 8.5 %collective-permute-start.11 = (bf16[2,64,1024]{2,1,0:T(8,128)(2,1)S(1)}, bf16[2,64,1024]{2,1,0:T(8,128)(2,1)S(1)}, u32[]{:S(2)}, u32[]{:S(2)}) collective-permute-start(bf16[2,64,1024]{2,1,0:T(8,128)(2,1)S(1)} %collective-permute-done.10), channel_id=1, source_target_pairs={{15,0},{0,1},{1,2},{2,3},{3,4},{4,5},{5,6},{6,7},{7,8},{8,9},{9,10... | collective-permute-start | bytes 786440 | tf_op jit(solution)/shard_map/ppermute | solution.py:13
  128.2 29.0 %collective-permute-start.15 = (bf16[64,1024]{1,0:T(8,128)(2,1)S(1)}, bf16[64,1024]{1,0:T(8,128)(2,1)S(1)}, u32[]{:S(2)}, u32[]{:S(2)}) collective-permute-start(bf16[64,1024]{1,0:T(8,128)(2,1)S(1)} %fusion.276), channel_id=1, source_target_pairs={{2,0},{3,1},{4,2},{5,3},{6,4},{7,5},{8,6},{9,7},{10,8},{11,9},{12,... | collective-permute-start | bytes 393224 | tf_op jit(solution)/shard_map/ppermute | solution.py:13
  129.0 27.4 %collective-permute-start.14 = (bf16[64,1024]{1,0:T(8,128)(2,1)S(1)}, bf16[64,1024]{1,0:T(8,128)(2,1)S(1)}, u32[]{:S(2)}, u32[]{:S(2)}) collective-permute-start(bf16[64,1024]{1,0:T(8,128)(2,1)S(1)} %fusion.276), channel_id=1, source_target_pairs={{1,0},{2,1},{3,2},{4,3},{5,4},{6,5},{7,6},{8,7},{9,8},{10,9},{11,1... | collective-permute-start | bytes 393224 | tf_op jit(solution)/shard_map/ppermute | solution.py:13
  130.8 24.7 %collective-permute-start.13 = (bf16[64,1024]{1,0:T(8,128)(2,1)S(1)}, bf16[64,1024]{1,0:T(8,128)(2,1)S(1)}, u32[]{:S(2)}, u32[]{:S(2)}) collective-permute-start(bf16[64,1024]{1,0:T(8,128)(2,1)S(1)} %fusion.276), channel_id=1, source_target_pairs={{15,0},{0,1},{1,2},{2,3},{3,4},{4,5},{5,6},{6,7},{7,8},{8,9},{9,10... | collective-permute-start | bytes 393224 | tf_op jit(solution)/shard_map/ppermute | solution.py:13
  130.8 27.3 %collective-permute-start.12 = (bf16[64,1024]{1,0:T(8,128)(2,1)S(1)}, bf16[64,1024]{1,0:T(8,128)(2,1)S(1)}, u32[]{:S(2)}, u32[]{:S(2)}) collective-permute-start(bf16[64,1024]{1,0:T(8,128)(2,1)S(1)} %fusion.276), channel_id=1, source_target_pairs={{14,0},{15,1},{0,2},{1,3},{2,4},{3,5},{4,6},{5,7},{6,8},{7,9},{8,1... | collective-permute-start | bytes 393224 | tf_op jit(solution)/shard_map/ppermute | solution.py:13
  159.4 22.5 %collective-permute-start.16 = (bf16[2,64,1024]{2,1,0:T(8,128)(2,1)S(1)}, bf16[2,64,1024]{2,1,0:T(8,128)(2,1)S(1)}, u32[]{:S(2)}, u32[]{:S(2)}) collective-permute-start(bf16[2,64,1024]{2,1,0:T(8,128)(2,1)S(1)} %get-tuple-element.12), channel_id=1, source_target_pairs={{1,0},{2,1},{3,2},{4,3},{5,4},{6,5},{7,6},{8,7},{9,8},{10,9},{11,1... | collective-permute-start | bytes 786440 | tf_op jit(solution)/shard_map/ppermute | solution.py:13
  160.8 22.0 %collective-permute-start.18 = (bf16[2,64,1024]{2,1,0:T(8,128)(2,1)S(1)}, bf16[2,64,1024]{2,1,0:T(8,128)(2,1)S(1)}, u32[]{:S(2)}, u32[]{:S(2)}) collective-permute-start(bf16[2,64,1024]{2,1,0:T(8,128)(2,1)S(1)} %get-tuple-element.12), channel_id=1, source_target_pairs={{15,0},{0,1},{1,2},{2,3},{3,4},{4,5},{5,6},{6,7},{7,8},{8,9},{9,10... | collective-permute-start | bytes 786440 | tf_op jit(solution)/shard_map/ppermute | solution.py:13
  181.8 4.6 %collective-permute-start.17 = (bf16[2,64,1024]{2,1,0:T(8,128)(2,1)S(1)}, bf16[2,64,1024]{2,1,0:T(8,128)(2,1)S(1)}, u32[]{:S(2)}, u32[]{:S(2)}) collective-permute-start(bf16[2,64,1024]{2,1,0:T(8,128)(2,1)S(1)} %collective-permute-done.16), channel_id=1, source_target_pairs={{1,0},{2,1},{3,2},{4,3},{5,4},{6,5},{7,6},{8,7},{9,8},{10,9},{11,1... | collective-permute-start | bytes 786440 | tf_op jit(solution)/shard_map/ppermute | solution.py:13
  182.8 8.5 %collective-permute-start.19 = (bf16[2,64,1024]{2,1,0:T(8,128)(2,1)S(1)}, bf16[2,64,1024]{2,1,0:T(8,128)(2,1)S(1)}, u32[]{:S(2)}, u32[]{:S(2)}) collective-permute-start(bf16[2,64,1024]{2,1,0:T(8,128)(2,1)S(1)} %collective-permute-done.18), channel_id=1, source_target_pairs={{15,0},{0,1},{1,2},{2,3},{3,4},{4,5},{5,6},{6,7},{7,8},{8,9},{9,10... | collective-permute-start | bytes 786440 | tf_op jit(solution)/shard_map/ppermute | solution.py:13
  193.6 29.0 %collective-permute-start.23 = (bf16[64,1024]{1,0:T(8,128)(2,1)S(1)}, bf16[64,1024]{1,0:T(8,128)(2,1)S(1)}, u32[]{:S(2)}, u32[]{:S(2)}) collective-permute-start(bf16[64,1024]{1,0:T(8,128)(2,1)S(1)} %get-tuple-element.14), channel_id=1, source_target_pairs={{2,0},{3,1},{4,2},{5,3},{6,4},{7,5},{8,6},{9,7},{10,8},{11,9},{12,... | collective-permute-start | bytes 393224 | tf_op jit(solution)/shard_map/ppermute | solution.py:13
  194.3 27.4 %collective-permute-start.22 = (bf16[64,1024]{1,0:T(8,128)(2,1)S(1)}, bf16[64,1024]{1,0:T(8,128)(2,1)S(1)}, u32[]{:S(2)}, u32[]{:S(2)}) collective-permute-start(bf16[64,1024]{1,0:T(8,128)(2,1)S(1)} %get-tuple-element.14), channel_id=1, source_target_pairs={{1,0},{2,1},{3,2},{4,3},{5,4},{6,5},{7,6},{8,7},{9,8},{10,9},{11,1... | collective-permute-start | bytes 393224 | tf_op jit(solution)/shard_map/ppermute | solution.py:13
  196.1 24.7 %collective-permute-start.21 = (bf16[64,1024]{1,0:T(8,128)(2,1)S(1)}, bf16[64,1024]{1,0:T(8,128)(2,1)S(1)}, u32[]{:S(2)}, u32[]{:S(2)}) collective-permute-start(bf16[64,1024]{1,0:T(8,128)(2,1)S(1)} %get-tuple-element.14), channel_id=1, source_target_pairs={{15,0},{0,1},{1,2},{2,3},{3,4},{4,5},{5,6},{6,7},{7,8},{8,9},{9,10... | collective-permute-start | bytes 393224 | tf_op jit(solution)/shard_map/ppermute | solution.py:13
  196.2 27.3 %collective-permute-start.20 = (bf16[64,1024]{1,0:T(8,128)(2,1)S(1)}, bf16[64,1024]{1,0:T(8,128)(2,1)S(1)}, u32[]{:S(2)}, u32[]{:S(2)}) collective-permute-start(bf16[64,1024]{1,0:T(8,128)(2,1)S(1)} %get-tuple-element.14), channel_id=1, source_target_pairs={{14,0},{15,1},{0,2},{1,3},{2,4},{3,5},{4,6},{5,7},{6,8},{7,9},{8,1... | collective-permute-start | bytes 393224 | tf_op jit(solution)/shard_map/ppermute | solution.py:13
where the time goes:
time: 226 us; the launch traced here: 225 us
  blocking collectives  121 us (54%)
  matrix products  57.4 us (25%)
  starting transfers between devices  23.6 us (10%)
  between operations  11 us (5%)
  waiting for transfers between devices  8.53 us (4%)
    all_gather x3, blocking collectives, on_device(): lax.all_gather(data_summary[None], 'row', axis=0, tiled=True)  63.1 us
    all_gather x3, blocking collectives, on_device(): add_received = lax.all_gather(summary[None], 'row', axis=0, tiled=True)  58.2 us
    dot_general x15, matrix products, on_device(): jnp.einsum('lpc,lac->pa', received_map[shift_by], tile_list[offset_slot],...  33.9 us
    ppermute x24, starting transfers between devices, shifted(): return lax.ppermute(block, axis, route)  23.6 us
    dot_general x15, matrix products, on_device(): jnp.einsum('pa,lac->lpc', received, tile_list[offset_slot], preferred_ele...  14.2 us
    ppermute x24, waiting for transfers between devices, shifted(): return lax.ppermute(block, axis, route)  8.53 us
  transfers between devices with their start and end apart: 24, of which 4 were waited for; matrix products, arithmetic and copies ran while one was open for 22% of the time, Pallas kernels for 0%

commit v1 on v0

v1 whole, which is shorter than its diff:
```python
import functools

import jax
import jax.numpy as jnp
from jax import lax
from jax.experimental import pallas as pl
from jax.experimental.pallas import tpu as pltpu
from jax.sharding import PartitionSpec as P

RADIUS = 2
ITERS = 3
CHUNK = 512
HANDED, FAR, PARTNER, NEXT = range(4)
NT = (((1,), (1,)), ((), ()))
NN = (((1,), (0,)), ((), ()))


def mm(lhs, rhs, dims=NN):
    return lax.dot_general(lhs, rhs, dims, preferred_element_type=jnp.float32)


def kernel(
    n, order_ref, tiles_hbm, basis_ref, core_ref, initial_hbm, observed_hbm, model_ref, misfit_ref,
    tiles, initial_ref, observed_ref, initial_in, base, wire_cols, change_cols, misfit_wire,
    part_out, part_in, misfit_in, sent_part, held, arrived, near, sum_f, sum_b,
    tile_sem, small_sem, initial_send, initial_recv, gather_send, gather_recv, halo_send, halo_recv,
):
    layers, perts, points = model_ref.shape
    rank = sum_f.shape[1]
    lr = layers * rank
    me = lax.axis_index("row")
    out = 2 * lax.rem(me, 2) - 1
    small = [
        pltpu.make_async_copy(initial_hbm, initial_ref, small_sem.at[0]),
        pltpu.make_async_copy(observed_hbm, observed_ref, small_sem.at[1]),
    ]
    for load in small:
        load.start()
    loads = [
        pltpu.make_async_copy(tiles_hbm.at[l, k], tiles.at[l, k], tile_sem.at[l, k])
        for l in range(layers)
        for k in range(tiles.shape[1])
    ]
    for load in loads:
        load.start()

    barrier = pltpu.get_barrier_semaphore()

    def greet(d, carry):
        pl.semaphore_signal(
            barrier, inc=1, device_id={"row": lax.rem(me + d, n)}, device_id_type=pl.DeviceIdType.MESH
        )
        return carry

    lax.fori_loop(1, n, greet, 0)
    pl.semaphore_wait(barrier, n - 1)

    slot_of = []
    for o in range(-RADIUS, RADIUS + 1):
        found = jnp.int32(0)
        for k in range(2 * RADIUS + 1):
            found = jnp.maximum(found, jnp.where(order_ref[k] == o + RADIUS, k, 0))
        slot_of.append(found)

    def tile_slot(steps):
        return jnp.where(out > 0, slot_of[RADIUS + steps], slot_of[RADIUS - steps])

    row = lax.broadcasted_iota(jnp.int32, (lr, layers * perts), 0)
    lane = lax.broadcasted_iota(jnp.int32, (lr, layers * perts), 1)
    same_layer = (row // rank) == (lane // perts)

    def pick(full):
        kept = jnp.where(same_layer, full, 0.0)
        return sum(kept[l * rank : (l + 1) * rank] for l in range(layers))

    def gather_copy(buf, which, d, sign):
        return pltpu.make_async_remote_copy(
            src_ref=buf.at[0],
            dst_ref=buf.at[d],
            send_sem=gather_send.at[which],
            recv_sem=gather_recv.at[which],
            device_id={"row": lax.rem(me + sign * d + n, n)},
            device_id_type=pl.DeviceIdType.MESH,
        )

    def gather_start(buf, which, sign):
        def send(d, carry):
            gather_copy(buf, which, d, sign).start()
            return carry

        lax.fori_loop(1, n, send, 0)

    def gather_all(buf, which):
        return pltpu.make_async_remote_copy(
            src_ref=buf.at[pl.ds(1, n - 1)],
            dst_ref=buf.at[pl.ds(1, n - 1)],
            send_sem=gather_send.at[which],
            recv_sem=gather_recv.at[which],
            device_id={"row": lax.rem(me + 1, n)},
            device_id_type=pl.DeviceIdType.MESH,
        )

    def halo(src, dst, which, at, j, steps):
        return pltpu.make_async_remote_copy(
            src_ref=src,
            dst_ref=dst.at[at, j],
            send_sem=halo_send.at[which, at, j],
            recv_sem=halo_recv.at[which, at, j],
            device_id={"row": lax.rem(me + steps * out + n, n)},
            device_id_type=pl.DeviceIdType.MESH,
        )

    def spread(total, which):
        packed = total.reshape(n * rank, layers * perts)
        both = sum(mm(core_ref[which], part) for part in split(packed))
        return split(jnp.where(same_layer, both[:lr] + both[lr:], 0.0).T)

    def split(value):
        if value.dtype == jnp.bfloat16:
            return (value,)
        high = value.astype(jnp.bfloat16)
        return high, (value - high.astype(jnp.float32)).astype(jnp.bfloat16)

    chunks = points // CHUNK
    columns = [pl.ds(j * CHUNK, CHUNK) for j in range(chunks)]

    def upright(value):
        return value.astype(jnp.float32).T.astype(jnp.bfloat16)

    def forward(cells, steps, j):
        return sum(
            mm(tiles[l, tile_slot(steps), columns[j], :], cells[l]) for l in range(layers)
        ).T

    def initial(src, at, l, steps):
        return pltpu.make_async_remote_copy(
            src_ref=src,
            dst_ref=initial_in.at[at, l],
            send_sem=initial_send.at[at, l],
            recv_sem=initial_recv.at[at, l],
            device_id={"row": lax.rem(me + steps * out + n, n)},
            device_id_type=pl.DeviceIdType.MESH,
        )

    def send_part(at, j, steps, value):
        change = (value - sent_part[at, j]).astype(jnp.bfloat16)
        sent_part[at, j] += change.astype(jnp.float32)
        part_out[at, j] = change
        halo(part_out.at[at, j], part_in, 0, at, j, steps).start()

    def backward(source, at):
        value = jnp.concatenate([source[j] for j in range(chunks)], 1)
        for l in range(layers):
            for cols in columns:
                near[l, :, cols] += mm(value, tiles[l, at, :, cols])

    for load in small:
        load.wait()
    for l in range(layers):
        for at, steps in ((NEXT, 1), (FAR, -2), (PARTNER, -1)):
            initial(initial_ref.at[l], at, l, steps).start()
    model_ref[...] = initial_ref[...].astype(jnp.float32)
    for l in range(layers):
        base[l] = upright(initial_ref[l])
    sent_part[...] = jnp.zeros_like(sent_part)
    held[...] = jnp.zeros_like(held)
    arrived[...] = jnp.zeros_like(arrived)

    def step(index, carry):
        model_wire = model_ref[...].astype(jnp.bfloat16)
        sum_f[0] = pick(mm(basis_ref[1], model_wire.reshape(layers * perts, points), NT))
        gather_start(sum_f, 0, 1)
        for l in range(layers):
            wire_cols[l] = upright(model_wire[l])
            change_cols[l] = wire_cols[l] - base[l]

        @pl.when(index == 0)
        def _():
            for l in range(layers):
                initial(initial_ref.at[l], NEXT, l, 1).wait_recv()
                initial(initial_in.at[NEXT, l], HANDED, l, -1).start()
            for load in loads:
                load.wait()
            for at, steps in ((PARTNER, 1), (NEXT, -1), (FAR, -2), (HANDED, 2)):
                if at != NEXT:
                    for l in range(layers):
                        initial(initial_ref.at[l], at, l, 1).wait_recv()
                cells = [upright(initial_in[at, l]) for l in range(layers)]
                for j in range(chunks):
                    arrived[j] += forward(cells, steps, j)
            for at in (HANDED, FAR, PARTNER, NEXT):
                for l in range(layers):
                    initial(initial_ref.at[l], at, l, 1).wait_send()

        @pl.when(index > 0)
        def _():
            for j in range(chunks):
                send_part(HANDED, j, -1, forward(change_cols, -2, j))
                send_part(FAR, j, 2, forward(change_cols, 2, j))
                send_part(PARTNER, j, -1, forward(change_cols, -1, j))
                beside = forward(change_cols, 1, j)
                halo(part_out.at[HANDED, j], part_in, 0, HANDED, j, -1).wait_recv()
                held[j] += part_in[HANDED, j].astype(jnp.float32)
                send_part(NEXT, j, 1, beside + held[j])

        gather_all(sum_f, 0).wait_recv()
        weights = spread(sum_f[...], 0)
        for j in range(chunks):
            both = sum(mm(part, basis_ref[0, :, columns[j]]) for part in weights)
            predicted = forward(wire_cols, 0, j) + sum(
                both[l * perts : (l + 1) * perts] for l in range(layers)
            )

            @pl.when(index > 0)
            def _():
                total = arrived[j]
                for at, steps in ((PARTNER, -1), (NEXT, 1), (FAR, 2)):
                    halo(part_out.at[at, j], part_in, 0, at, j, steps).wait_recv()
                    total = total + part_in[at, j].astype(jnp.float32)
                arrived[j] = total

            misfit = observed_ref[:, columns[j]].astype(jnp.float32) - (predicted + arrived[j])
            misfit_ref[:, columns[j]] = misfit
            misfit_wire[j] = misfit.astype(jnp.bfloat16)
            for at, steps in ((NEXT, 1), (FAR, -2), (PARTNER, -1)):
                halo(misfit_wire.at[j], misfit_in, 1, at, j, steps).start()

        wire = jnp.concatenate([misfit_wire[j] for j in range(chunks)], 1)
        sum_b[0] = pick(
            mm(basis_ref[0], jnp.concatenate([wire] * layers, 0), NT)
        )
        gather_start(sum_b, 1, -1)
        for l in range(layers):
            for cols in columns:
                near[l, :, cols] = mm(wire, tiles[l, tile_slot(0), :, cols])

        def relay(j):
            halo(misfit_wire.at[j], misfit_in, 1, NEXT, j, 1).wait_recv()
            halo(misfit_in.at[NEXT, j], misfit_in, 1, HANDED, j, -1).start()

        def received(at, steps):
            for j in range(chunks):
                halo(misfit_wire.at[j], misfit_in, 1, at, j, steps).wait_recv()

        for j in range(chunks // 2):
            relay(j)
        received(PARTNER, -1)
        backward(misfit_in.at[PARTNER], tile_slot(-1))
        for j in range(chunks // 2, chunks):
            relay(j)
        backward(misfit_in.at[NEXT], tile_slot(1))
        received(FAR, -2)
        backward(misfit_in.at[FAR], tile_slot(2))
        gather_all(sum_b, 1).wait_recv()
        near[...] += sum(
            mm(part, basis_ref[1]) for part in spread(sum_b[...], 1)
        ).reshape(layers, perts, points)
        received(HANDED, -1)
        backward(misfit_in.at[HANDED], tile_slot(-2))
        model = model_ref[...]
        model_ref[...] = model + 0.01 * (near[...] - 10.0 * model)
        for j in range(chunks):
            for at in (HANDED, FAR, PARTNER, NEXT):
                halo(misfit_wire.at[j], misfit_in, 1, at, j, 1).wait_send()

        @pl.when(index > 0)
        def _():
            for j in range(chunks):
                for at in (HANDED, FAR, PARTNER, NEXT):
                    halo(part_out.at[at, j], part_in, 0, at, j, 1).wait_send()

        gather_all(sum_f, 0).wait_send()
        gather_all(sum_b, 1).wait_send()
        return carry

    lax.fori_loop(0, ITERS, step, 0)


def on_device(
    n, near_tiles, near_order, receiver_basis, source_basis, coupling, initial_model, observed
):
    layers, span, points, _ = near_tiles.shape
    rank = receiver_basis.shape[-1]
    perts = observed.shape[0]
    basis = jnp.stack([receiver_basis, source_basis]).transpose(0, 1, 3, 2)
    basis = basis.reshape(2, layers * rank, points)
    ahead = coupling.transpose(0, 2, 1, 3).reshape(layers * rank, n * rank)
    back = coupling.transpose(0, 3, 1, 2).reshape(layers * rank, n * rank)
    core = jnp.stack([ahead, back])
    high = lax.reduce_precision(core, 8, 7)
    core = jnp.concatenate([high, core - high], 1).astype(jnp.bfloat16)
    vmem = pl.BlockSpec(memory_space=pltpu.VMEM)
    chunks = points // CHUNK
    return pl.pallas_call(
        functools.partial(kernel, n),
        out_shape=(
            jax.ShapeDtypeStruct((layers, perts, points), jnp.float32),
            jax.ShapeDtypeStruct((perts, points), jnp.float32),
        ),
        in_specs=[
            pl.BlockSpec(memory_space=pltpu.SMEM),
            pl.BlockSpec(memory_space=pltpu.HBM),
            vmem,
            vmem,
            pl.BlockSpec(memory_space=pltpu.HBM),
            pl.BlockSpec(memory_space=pltpu.HBM),
        ],
        out_specs=(vmem, vmem),
        scratch_shapes=[
            pltpu.VMEM(near_tiles.shape, jnp.bfloat16),
            pltpu.VMEM((layers, perts, points), jnp.bfloat16),
            pltpu.VMEM((perts, points), jnp.bfloat16),
            pltpu.VMEM((4, layers, perts, points), jnp.bfloat16),
            pltpu.VMEM((layers, points, perts), jnp.bfloat16),
            pltpu.VMEM((layers, points, perts), jnp.bfloat16),
            pltpu.VMEM((layers, points, perts), jnp.bfloat16),
            pltpu.VMEM((chunks, perts, CHUNK), jnp.bfloat16),
            pltpu.VMEM((4, chunks, perts, CHUNK), jnp.bfloat16),
            pltpu.VMEM((4, chunks, perts, CHUNK), jnp.bfloat16),
            pltpu.VMEM((4, chunks, perts, CHUNK), jnp.bfloat16),
            pltpu.VMEM((4, chunks, perts, CHUNK), jnp.float32),
            pltpu.VMEM((chunks, perts, CHUNK), jnp.float32),
            pltpu.VMEM((chunks, perts, CHUNK), jnp.float32),
            pltpu.VMEM((layers, perts, points), jnp.float32),
            pltpu.VMEM((n, rank, layers * perts), jnp.float32),
            pltpu.VMEM((n, rank, layers * perts), jnp.float32),
            pltpu.SemaphoreType.DMA((layers, span)),
            pltpu.SemaphoreType.DMA((2,)),
            pltpu.SemaphoreType.DMA((4, layers)),
            pltpu.SemaphoreType.DMA((4, layers)),
            pltpu.SemaphoreType.DMA((2,)),
            pltpu.SemaphoreType.DMA((2,)),
            pltpu.SemaphoreType.DMA((2, 4, chunks)),
            pltpu.SemaphoreType.DMA((2, 4, chunks)),
        ],
        compiler_params=pltpu.CompilerParams(
            collective_id=0, has_side_effects=True, vmem_limit_bytes=63 * 2**20
        ),
    )(near_order, near_tiles, basis, core, initial_model, observed)


def solution(mesh):
    placed = (P(), P(), P(), P(), P(), P(None, "group", "row"), P("group", "row"))
    return jax.shard_map(
        functools.partial(on_device, mesh.shape["row"]),
        mesh=mesh,
        in_specs=placed,
        out_specs=(P(None, "group", "row"), P("group", "row")),
        check_vma=False,
    )
```

time: 226 us -> 98 us (0.43)
  blocking collectives: 121 us -> 0 us
  Pallas kernels: 0 us -> 88.5 us
  matrix products: 57.4 us -> 0 us
  starting transfers between devices: 23.6 us -> 0 us
  between operations: 11 us -> 0.66 us
  waiting for transfers between devices: 8.53 us -> 0 us
  local copies, waits for them, and re-layouts: 1.84 us -> 6 us
    all_gather x6 -> x0, blocking collectives: 121 us -> none  [the longest x3 63.1 us: on_device(): lax.all_gather(data_summary[None], 'row', axis=0, tiled=True)]
    pallas_call x0 -> x1, Pallas kernels: none -> 88.5 us  [on_device(): pl.pallas_call(functools.partial(kernel, n), out_shape=(jax.ShapeDtypeStr...]
    dot_general x45 -> x0, matrix products: 56.9 us -> none  [the longest x15 33.9 us: on_device(): jnp.einsum('lpc,lac->pa', received_map[shift_by], tile_list[offset_slot],...]
    ppermute x24 -> x0, starting transfers between devices: 23.6 us -> none  [shifted(): return lax.ppermute(block, axis, route)]
    ppermute x24 -> x0, waiting for transfers between devices: 8.53 us -> none  [shifted(): return lax.ppermute(block, axis, route)]
    unnamed x12 -> x3, local copies, waits for them, and re-layouts: 0.04 us -> 3.56 us
  transfers between devices with their start and end apart: 24 -> 0, of which waited for: 4 -> 0; matrix products, arithmetic and copies ran while one was open for 22% -> 0% of each run, Pallas kernels for 0% -> 0%
where the time goes in v1:
time: 98 us; the launch traced here: 97.4 us
  Pallas kernels  88.5 us (90%)
  local copies, waits for them, and re-layouts  6 us (6%)
  other arithmetic  2.19 us (2%)
    pallas_call x1, Pallas kernels, on_device(): pl.pallas_call(functools.partial(kernel, n), out_shape=(jax.ShapeDtypeStr...  88.5 us
    unnamed x3, local copies, waits for them, and re-layouts  3.56 us

profile of v1, /device:TPU:0, one launch (start us, length us, event | category | flops | bytes accessed | tf_op | source)
XLA Modules:
  0.0 97.4 jit_solution(15456844683071664985)
XLA Ops:
  0.6 1.5 %pad_maximum_fusion = bf16[2,2,1024,16]{2,3,1,0:T(8,128)(2,1)} fusion(bf16[1,2,1024,16]{2,3,1,0:T(8,128)(2,1)} %bitcast.14, bf16[1,2,1024,16]{2,3,1,0:T(8,128)(2,1)} %bitcast.15), kind=kLoop, calls=%fused_computation | loop fusion | flops 65536 | bytes 262144 | tf_op jit(solution)/shard_map/stack | solution.py:285
  2.2 1.0 %copy.9 = f32[2,16,16,16]{3,2,1,0:T(8,128)S(1)} copy(f32[2,16,16,16]{3,1,2,0:T(8,128)} %bitcast.11) | data formatting | bytes 65536 | tf_op jit(solution)/shard_map/transpose | solution.py:287
  3.2 0.1 stack_reshape.6
  3.4 1.1 %copy.10 = f32[2,16,16,16]{3,2,1,0:T(8,128)S(1)} copy(f32[2,16,16,16]{1,3,2,0:T(8,128)} %bitcast.12) | data formatting | bytes 65536 | tf_op jit(solution)/shard_map/transpose | solution.py:288
  4.5 0.1 stack_reshape.7
  4.7 0.6 pad_maximum_fusion.1.core_ref
  5.3 88.5 %shard_map.86 = (f32[2,64,1024]{2,1,0:T(8,128)}, f32[64,1024]{1,0:T(8,128)}) custom-call(s32[5]{0:T(128)} %order_ref.1, bf16[2,5,1024,1024]{3,2,1,0:T(8,128)(2,1)} %tiles_hbm.1, bf16[2,32,1024]{2,1,0:T(8,128)(2,1)} %bitcast.13, bf16[2,64,256]{2,1,0:T(8,128)(2,1)} %pad_maximum_fusion.1.core_ref, bf16[2,64,1024]{2,1,0:T(8,128)(2,1)} %initial_hbm.1, ...), custom_call_target="tpu_custom_call" | custom-call | tf_op jit(solution)/shard_map/pallas_call | solution.py:294
  93.8 1.9 %copy.14 = f32[2,64,1024]{2,1,0:T(8,128)} copy(f32[2,64,1024]{2,1,0:T(8,128)} %get-tuple-element.6) | data formatting | bytes 1048576
  95.7 1.7 %copy.15 = f32[64,1024]{1,0:T(8,128)} copy(f32[64,1024]{1,0:T(8,128)} %get-tuple-element.7) | data formatting | bytes 524288
  (3 shorter events, 0.0 us)

commit v2 on v1

--- a/solution.py
+++ b/solution.py
@@ -20,8 +20,8 @@
 
 
 def kernel(
-    n, order_ref, tiles_hbm, basis_ref, core_ref, initial_hbm, observed_hbm, model_ref, misfit_ref,
-    tiles, initial_ref, observed_ref, initial_in, base, wire_cols, change_cols, misfit_wire,
+    n, order_ref, tiles_hbm, receiver_hbm, source_hbm, coupling_hbm, initial_hbm, observed_hbm,
+    model_ref, misfit_ref, tiles, basis_in, coupling_in, core_ref, initial_ref, observed_ref, initial_in, wire, change, misfit_wire,
     part_out, part_in, misfit_in, sent_part, held, arrived, near, sum_f, sum_b,
     tile_sem, small_sem, initial_send, initial_recv, gather_send, gather_recv, halo_send, halo_recv,
 ):
@@ -33,6 +33,9 @@
     small = [
         pltpu.make_async_copy(initial_hbm, initial_ref, small_sem.at[0]),
         pltpu.make_async_copy(observed_hbm, observed_ref, small_sem.at[1]),
+        pltpu.make_async_copy(receiver_hbm, basis_in.at[0], small_sem.at[2]),
+        pltpu.make_async_copy(source_hbm, basis_in.at[1], small_sem.at[3]),
+        pltpu.make_async_copy(coupling_hbm, coupling_in, small_sem.at[4]),
     ]
     for load in small:
         load.start()
@@ -69,6 +72,9 @@
     lane = lax.broadcasted_iota(jnp.int32, (lr, layers * perts), 1)
     same_layer = (row // rank) == (lane // perts)
 
+    def basis(side):
+        return basis_in[side].reshape(lr, points)
+
     def pick(full):
         kept = jnp.where(same_layer, full, 0.0)
         return sum(kept[l * rank : (l + 1) * rank] for l in range(layers))
@@ -124,13 +130,10 @@
     chunks = points // CHUNK
     columns = [pl.ds(j * CHUNK, CHUNK) for j in range(chunks)]
 
-    def upright(value):
-        return value.astype(jnp.float32).T.astype(jnp.bfloat16)
-
     def forward(cells, steps, j):
         return sum(
-            mm(tiles[l, tile_slot(steps), columns[j], :], cells[l]) for l in range(layers)
-        ).T
+            mm(cells[l], tiles[l, tile_slot(steps), columns[j], :], NT) for l in range(layers)
+        )
 
     def initial(src, at, l, steps):
         return pltpu.make_async_remote_copy(
@@ -161,18 +164,23 @@
             initial(initial_ref.at[l], at, l, steps).start()
     model_ref[...] = initial_ref[...].astype(jnp.float32)
     for l in range(layers):
-        base[l] = upright(initial_ref[l])
+        rows = pl.ds(l * rank, rank)
+        ahead = jnp.concatenate([coupling_in[l, d] for d in range(n)], 1)
+        back = jnp.concatenate([coupling_in[l, d].T for d in range(n)], 1)
+        for which, core in enumerate((ahead, back)):
+            high, low = split(core)
+            core_ref[which, rows, :] = high
+            core_ref[which, pl.ds(lr + l * rank, rank), :] = low
     sent_part[...] = jnp.zeros_like(sent_part)
     held[...] = jnp.zeros_like(held)
     arrived[...] = jnp.zeros_like(arrived)
 
     def step(index, carry):
         model_wire = model_ref[...].astype(jnp.bfloat16)
-        sum_f[0] = pick(mm(basis_ref[1], model_wire.reshape(layers * perts, points), NT))
+        sum_f[0] = pick(mm(basis(1), model_wire.reshape(layers * perts, points), NT))
         gather_start(sum_f, 0, 1)
-        for l in range(layers):
-            wire_cols[l] = upright(model_wire[l])
-            change_cols[l] = wire_cols[l] - base[l]
+        wire[...] = model_wire
+        change[...] = model_wire - initial_ref[...]
 
         @pl.when(index == 0)
         def _():
@@ -185,7 +193,7 @@
                 if at != NEXT:
                     for l in range(layers):
                         initial(initial_ref.at[l], at, l, 1).wait_recv()
-                cells = [upright(initial_in[at, l]) for l in range(layers)]
+                cells = initial_in.at[at]
                 for j in range(chunks):
                     arrived[j] += forward(cells, steps, j)
             for at in (HANDED, FAR, PARTNER, NEXT):
@@ -195,10 +203,10 @@
         @pl.when(index > 0)
         def _():
             for j in range(chunks):
-                send_part(HANDED, j, -1, forward(change_cols, -2, j))
-                send_part(FAR, j, 2, forward(change_cols, 2, j))
-                send_part(PARTNER, j, -1, forward(change_cols, -1, j))
-                beside = forward(change_cols, 1, j)
+                send_part(HANDED, j, -1, forward(change, -2, j))
+                send_part(FAR, j, 2, forward(change, 2, j))
+                send_part(PARTNER, j, -1, forward(change, -1, j))
+                beside = forward(change, 1, j)
                 halo(part_out.at[HANDED, j], part_in, 0, HANDED, j, -1).wait_recv()
                 held[j] += part_in[HANDED, j].astype(jnp.float32)
                 send_part(NEXT, j, 1, beside + held[j])
@@ -206,8 +214,8 @@
         gather_all(sum_f, 0).wait_recv()
         weights = spread(sum_f[...], 0)
         for j in range(chunks):
-            both = sum(mm(part, basis_ref[0, :, columns[j]]) for part in weights)
-            predicted = forward(wire_cols, 0, j) + sum(
+            both = sum(mm(part, basis(0)[:, j * CHUNK : (j + 1) * CHUNK]) for part in weights)
+            predicted = forward(wire, 0, j) + sum(
                 both[l * perts : (l + 1) * perts] for l in range(layers)
             )
 
@@ -225,14 +233,14 @@
             for at, steps in ((NEXT, 1), (FAR, -2), (PARTNER, -1)):
                 halo(misfit_wire.at[j], misfit_in, 1, at, j, steps).start()
 
-        wire = jnp.concatenate([misfit_wire[j] for j in range(chunks)], 1)
+        data = jnp.concatenate([misfit_wire[j] for j in range(chunks)], 1)
         sum_b[0] = pick(
-            mm(basis_ref[0], jnp.concatenate([wire] * layers, 0), NT)
+            mm(basis(0), jnp.concatenate([data] * layers, 0), NT)
         )
         gather_start(sum_b, 1, -1)
         for l in range(layers):
             for cols in columns:
-                near[l, :, cols] = mm(wire, tiles[l, tile_slot(0), :, cols])
+                near[l, :, cols] = mm(data, tiles[l, tile_slot(0), :, cols])
 
         def relay(j):
             halo(misfit_wire.at[j], misfit_in, 1, NEXT, j, 1).wait_recv()
@@ -253,7 +261,7 @@
         backward(misfit_in.at[FAR], tile_slot(2))
         gather_all(sum_b, 1).wait_recv()
         near[...] += sum(
-            mm(part, basis_ref[1]) for part in spread(sum_b[...], 1)
+            mm(part, basis(1)) for part in spread(sum_b[...], 1)
         ).reshape(layers, perts, points)
         received(HANDED, -1)
         backward(misfit_in.at[HANDED], tile_slot(-2))
@@ -282,15 +290,14 @@
     layers, span, points, _ = near_tiles.shape
     rank = receiver_basis.shape[-1]
     perts = observed.shape[0]
-    basis = jnp.stack([receiver_basis, source_basis]).transpose(0, 1, 3, 2)
-    basis = basis.reshape(2, layers * rank, points)
-    ahead = coupling.transpose(0, 2, 1, 3).reshape(layers * rank, n * rank)
-    back = coupling.transpose(0, 3, 1, 2).reshape(layers * rank, n * rank)
-    core = jnp.stack([ahead, back])
-    high = lax.reduce_precision(core, 8, 7)
-    core = jnp.concatenate([high, core - high], 1).astype(jnp.bfloat16)
     vmem = pl.BlockSpec(memory_space=pltpu.VMEM)
     chunks = points // CHUNK
+    fixed = [
+        pltpu.with_memory_space_constraint(value, pltpu.HBM)
+        for value in (
+            receiver_basis.transpose(0, 2, 1), source_basis.transpose(0, 2, 1), coupling, initial_model, observed,
+        )
+    ]
     return pl.pallas_call(
         functools.partial(kernel, n),
         out_shape=(
@@ -299,21 +306,19 @@
         ),
         in_specs=[
             pl.BlockSpec(memory_space=pltpu.SMEM),
-            pl.BlockSpec(memory_space=pltpu.HBM),
-            vmem,
-            vmem,
-            pl.BlockSpec(memory_space=pltpu.HBM),
-            pl.BlockSpec(memory_space=pltpu.HBM),
+            *[pl.BlockSpec(memory_space=pltpu.HBM)] * 6,
         ],
         out_specs=(vmem, vmem),
         scratch_shapes=[
             pltpu.VMEM(near_tiles.shape, jnp.bfloat16),
+            pltpu.VMEM((2, layers, rank, points), jnp.bfloat16),
+            pltpu.VMEM(coupling.shape, jnp.float32),
+            pltpu.VMEM((2, 2 * layers * rank, n * rank), jnp.bfloat16),
             pltpu.VMEM((layers, perts, points), jnp.bfloat16),
             pltpu.VMEM((perts, points), jnp.bfloat16),
             pltpu.VMEM((4, layers, perts, points), jnp.bfloat16),
-            pltpu.VMEM((layers, points, perts), jnp.bfloat16),
-            pltpu.VMEM((layers, points, perts), jnp.bfloat16),
-            pltpu.VMEM((layers, points, perts), jnp.bfloat16),
+            pltpu.VMEM((layers, perts, points), jnp.bfloat16),
+            pltpu.VMEM((layers, perts, points), jnp.bfloat16),
             pltpu.VMEM((chunks, perts, CHUNK), jnp.bfloat16),
             pltpu.VMEM((4, chunks, perts, CHUNK), jnp.bfloat16),
             pltpu.VMEM((4, chunks, perts, CHUNK), jnp.bfloat16),
@@ -325,7 +330,7 @@
             pltpu.VMEM((n, rank, layers * perts), jnp.float32),
             pltpu.VMEM((n, rank, layers * perts), jnp.float32),
             pltpu.SemaphoreType.DMA((layers, span)),
-            pltpu.SemaphoreType.DMA((2,)),
+            pltpu.SemaphoreType.DMA((5,)),
             pltpu.SemaphoreType.DMA((4, layers)),
             pltpu.SemaphoreType.DMA((4, layers)),
             pltpu.SemaphoreType.DMA((2,)),
@@ -334,9 +339,11 @@
             pltpu.SemaphoreType.DMA((2, 4, chunks)),
         ],
         compiler_params=pltpu.CompilerParams(
-            collective_id=0, has_side_effects=True, vmem_limit_bytes=63 * 2**20
+            collective_id=0, has_side_effects=True, vmem_limit_bytes=52 * 2**20
         ),
-    )(near_order, near_tiles, basis, core, initial_model, observed)
+    )(
+        near_order, near_tiles, *fixed
+    )
 
 
 def solution(mesh):

time: 98 us -> 83.7 us (0.85)
  Pallas kernels: 88.5 us -> 80.7 us
  local copies, waits for them, and re-layouts: 6 us -> 2.15 us
  other arithmetic: 2.19 us -> 0 us
    pallas_call x1, Pallas kernels: 88.5 us -> 80.7 us  [on_device(): pl.pallas_call(functools.partial(kernel, n), out_shape=(jax.ShapeDtypeStr...]
    transpose x2 -> x0, local copies, waits for them, and re-layouts: 2.14 us -> none  [the longest x1 1.11 us: on_device(): back = coupling.transpose(0, 3, 1, 2).reshape(layers * rank, n * rank)]
    another operation x2 -> x0, other arithmetic: 1.55 us -> none  [the longest x1 1.54 us: on_device(): basis = jnp.stack([receiver_basis, source_basis]).transpose(0, 1, 3, 2)]
    unnamed x3 -> x4, local copies, waits for them, and re-layouts: 3.56 us -> 2.15 us
where the time goes in v2:
time: 83.7 us; the launch traced here: 83.5 us
  Pallas kernels  80.7 us (96%)
  local copies, waits for them, and re-layouts  2.15 us (3%)
    pallas_call x1, Pallas kernels, on_device(): pl.pallas_call(functools.partial(kernel, n), out_shape=(jax.ShapeDtypeStr...  80.7 us
    unnamed x4, local copies, waits for them, and re-layouts  2.15 us

profile of v2, /device:TPU:0, one launch (start us, length us, event | category | flops | bytes accessed | tf_op | source)
XLA Modules:
  0.0 83.5 jit_solution(3548174749369766687)
XLA Ops:
  0.6 0.0 copy-start
  0.6 0.6 copy-done
  1.3 80.7 %shard_map.86 = (f32[2,64,1024]{2,1,0:T(8,128)S(1)}, f32[64,1024]{1,0:T(8,128)S(1)}) custom-call(s32[5]{0:T(128)S(1)} %copy-done, bf16[2,5,1024,1024]{3,2,1,0:T(8,128)(2,1)} %tiles_hbm.1, bf16[2,16,1024]{2,1,0:T(8,128)(2,1)} %bitcast.2, bf16[2,16,1024]{2,1,0:T(8,128)(2,1)} %bitcast.3, f32[2,16,16,16]{3,2,1,0:T(8,128)} %coupling_hbm.1, ...), custom_call_target="tpu_custom_call" | custom-call | tf_op jit(solution)/shard_map/pallas_call | solution.py:301
  82.0 0.8 copy.11
  82.8 0.7 copy.12
Async XLA Ops:
  0.6 0.7 copy-start

commit v3 on v2

--- a/solution.py
+++ b/solution.py
@@ -49,9 +49,13 @@
 
     barrier = pltpu.get_barrier_semaphore()
 
+    def wrap(band):
+        band = jnp.where(band >= n, band - n, band)
+        return jnp.where(band < 0, band + n, band)
+
     def greet(d, carry):
         pl.semaphore_signal(
-            barrier, inc=1, device_id={"row": lax.rem(me + d, n)}, device_id_type=pl.DeviceIdType.MESH
+            barrier, inc=1, device_id={"row": wrap(me + d)}, device_id_type=pl.DeviceIdType.MESH
         )
         return carry
 
@@ -85,7 +89,7 @@
             dst_ref=buf.at[d],
             send_sem=gather_send.at[which],
             recv_sem=gather_recv.at[which],
-            device_id={"row": lax.rem(me + sign * d + n, n)},
+            device_id={"row": wrap(me + sign * d)},
             device_id_type=pl.DeviceIdType.MESH,
         )
 
@@ -102,7 +106,7 @@
             dst_ref=buf.at[pl.ds(1, n - 1)],
             send_sem=gather_send.at[which],
             recv_sem=gather_recv.at[which],
-            device_id={"row": lax.rem(me + 1, n)},
+            device_id={"row": wrap(me + 1)},
             device_id_type=pl.DeviceIdType.MESH,
         )
 
@@ -112,7 +116,7 @@
             dst_ref=dst.at[at, j],
             send_sem=halo_send.at[which, at, j],
             recv_sem=halo_recv.at[which, at, j],
-            device_id={"row": lax.rem(me + steps * out + n, n)},
+            device_id={"row": wrap(me + steps * out)},
             device_id_type=pl.DeviceIdType.MESH,
         )
 
@@ -141,7 +145,7 @@
             dst_ref=initial_in.at[at, l],
             send_sem=initial_send.at[at, l],
             recv_sem=initial_recv.at[at, l],
-            device_id={"row": lax.rem(me + steps * out + n, n)},
+            device_id={"row": wrap(me + steps * out)},
             device_id_type=pl.DeviceIdType.MESH,
         )
 
@@ -160,8 +164,10 @@
     for load in small:
         load.wait()
     for l in range(layers):
-        for at, steps in ((NEXT, 1), (FAR, -2), (PARTNER, -1)):
+        for at, steps in ((NEXT, 1), (PARTNER, -1)):
             initial(initial_ref.at[l], at, l, steps).start()
+    for l in range(layers):
+        initial(initial_ref.at[l], FAR, l, -2).start()
     model_ref[...] = initial_ref[...].astype(jnp.float32)
     for l in range(layers):
         rows = pl.ds(l * rank, rank)
@@ -177,20 +183,29 @@
 
     def step(index, carry):
         model_wire = model_ref[...].astype(jnp.bfloat16)
-        sum_f[0] = pick(mm(basis(1), model_wire.reshape(layers * perts, points), NT))
-        gather_start(sum_f, 0, 1)
         wire[...] = model_wire
         change[...] = model_wire - initial_ref[...]
 
+        def own():
+            for j in range(chunks):
+                misfit_ref[:, columns[j]] = forward(wire, 0, j)
+
+        def summarize():
+            sum_f[0] = pick(mm(basis(1), model_wire.reshape(layers * perts, points), NT))
+            gather_start(sum_f, 0, 1)
+
         @pl.when(index == 0)
         def _():
+            summarize()
             for l in range(layers):
                 initial(initial_ref.at[l], NEXT, l, 1).wait_recv()
                 initial(initial_in.at[NEXT, l], HANDED, l, -1).start()
             for load in loads:
                 load.wait()
-            for at, steps in ((PARTNER, 1), (NEXT, -1), (FAR, -2), (HANDED, 2)):
-                if at != NEXT:
+            for at, steps in ((PARTNER, 1), (NEXT, -1), (HANDED, 2), (FAR, -2)):
+                if at == NEXT:
+                    own()
+                else:
                     for l in range(layers):
                         initial(initial_ref.at[l], at, l, 1).wait_recv()
                 cells = initial_in.at[at]
@@ -205,17 +220,20 @@
             for j in range(chunks):
                 send_part(HANDED, j, -1, forward(change, -2, j))
                 send_part(FAR, j, 2, forward(change, 2, j))
-                send_part(PARTNER, j, -1, forward(change, -1, j))
                 beside = forward(change, 1, j)
                 halo(part_out.at[HANDED, j], part_in, 0, HANDED, j, -1).wait_recv()
                 held[j] += part_in[HANDED, j].astype(jnp.float32)
                 send_part(NEXT, j, 1, beside + held[j])
+                send_part(PARTNER, j, -1, forward(change, -1, j))
+                if j == 0:
+                    summarize()
+            own()
 
         gather_all(sum_f, 0).wait_recv()
         weights = spread(sum_f[...], 0)
         for j in range(chunks):
             both = sum(mm(part, basis(0)[:, j * CHUNK : (j + 1) * CHUNK]) for part in weights)
-            predicted = forward(wire, 0, j) + sum(
+            predicted = misfit_ref[:, columns[j]] + sum(
                 both[l * perts : (l + 1) * perts] for l in range(layers)
             )
 
@@ -230,8 +248,10 @@
             misfit = observed_ref[:, columns[j]].astype(jnp.float32) - (predicted + arrived[j])
             misfit_ref[:, columns[j]] = misfit
             misfit_wire[j] = misfit.astype(jnp.bfloat16)
-            for at, steps in ((NEXT, 1), (FAR, -2), (PARTNER, -1)):
+            for at, steps in ((NEXT, 1), (PARTNER, -1)):
                 halo(misfit_wire.at[j], misfit_in, 1, at, j, steps).start()
+        for j in range(chunks):
+            halo(misfit_wire.at[j], misfit_in, 1, FAR, j, -2).start()
 
         data = jnp.concatenate([misfit_wire[j] for j in range(chunks)], 1)
         sum_b[0] = pick(
@@ -257,14 +277,14 @@
         for j in range(chunks // 2, chunks):
             relay(j)
         backward(misfit_in.at[NEXT], tile_slot(1))
-        received(FAR, -2)
-        backward(misfit_in.at[FAR], tile_slot(2))
+        received(HANDED, -1)
+        backward(misfit_in.at[HANDED], tile_slot(-2))
         gather_all(sum_b, 1).wait_recv()
         near[...] += sum(
             mm(part, basis(1)) for part in spread(sum_b[...], 1)
         ).reshape(layers, perts, points)
-        received(HANDED, -1)
-        backward(misfit_in.at[HANDED], tile_slot(-2))
+        received(FAR, -2)
+        backward(misfit_in.at[FAR], tile_slot(2))
         model = model_ref[...]
         model_ref[...] = model + 0.01 * (near[...] - 10.0 * model)
         for j in range(chunks):

time: 83.7 us -> 86.2 us (1.030)
  Pallas kernels: 80.7 us -> 83.2 us
    pallas_call x1, Pallas kernels: 80.7 us -> 83.2 us  [on_device(): pl.pallas_call(functools.partial(kernel, n), out_shape=(jax.ShapeDtypeStr...]
where the time goes in v3:
time: 86.2 us; the launch traced here: 86 us
  Pallas kernels  83.2 us (97%)
  local copies, waits for them, and re-layouts  2.15 us (2%)
    pallas_call x1, Pallas kernels, on_device(): pl.pallas_call(functools.partial(kernel, n), out_shape=(jax.ShapeDtypeStr...  83.2 us
    unnamed x4, local copies, waits for them, and re-layouts  2.15 us

profile of v3, /device:TPU:0, one launch (start us, length us, event | category | flops | bytes accessed | tf_op | source)
XLA Modules:
  0.0 86.0 jit_solution(7257118086867831009)
XLA Ops:
  0.6 0.0 copy-start
  0.6 0.6 copy-done
  1.3 83.2 %shard_map.86 = (f32[2,64,1024]{2,1,0:T(8,128)S(1)}, f32[64,1024]{1,0:T(8,128)S(1)}) custom-call(s32[5]{0:T(128)S(1)} %copy-done, bf16[2,5,1024,1024]{3,2,1,0:T(8,128)(2,1)} %tiles_hbm.1, bf16[2,16,1024]{2,1,0:T(8,128)(2,1)} %bitcast.2, bf16[2,16,1024]{2,1,0:T(8,128)(2,1)} %bitcast.3, f32[2,16,16,16]{3,2,1,0:T(8,128)} %coupling_hbm.1, ...), custom_call_target="tpu_custom_call" | custom-call | tf_op jit(solution)/shard_map/pallas_call | solution.py:321
  84.5 0.8 copy.11
  85.3 0.7 copy.12
Async XLA Ops:
  0.6 0.7 copy-start

commit v4 on v3

--- a/solution.py
+++ b/solution.py
@@ -164,10 +164,8 @@
     for load in small:
         load.wait()
     for l in range(layers):
-        for at, steps in ((NEXT, 1), (PARTNER, -1)):
+        for at, steps in ((NEXT, 1), (FAR, -2), (PARTNER, -1)):
             initial(initial_ref.at[l], at, l, steps).start()
-    for l in range(layers):
-        initial(initial_ref.at[l], FAR, l, -2).start()
     model_ref[...] = initial_ref[...].astype(jnp.float32)
     for l in range(layers):
         rows = pl.ds(l * rank, rank)
@@ -194,15 +192,16 @@
             sum_f[0] = pick(mm(basis(1), model_wire.reshape(layers * perts, points), NT))
             gather_start(sum_f, 0, 1)
 
+        summarize()
+
         @pl.when(index == 0)
         def _():
-            summarize()
             for l in range(layers):
                 initial(initial_ref.at[l], NEXT, l, 1).wait_recv()
                 initial(initial_in.at[NEXT, l], HANDED, l, -1).start()
             for load in loads:
                 load.wait()
-            for at, steps in ((PARTNER, 1), (NEXT, -1), (HANDED, 2), (FAR, -2)):
+            for at, steps in ((PARTNER, 1), (NEXT, -1), (FAR, -2), (HANDED, 2)):
                 if at == NEXT:
                     own()
                 else:
@@ -225,8 +224,6 @@
                 held[j] += part_in[HANDED, j].astype(jnp.float32)
                 send_part(NEXT, j, 1, beside + held[j])
                 send_part(PARTNER, j, -1, forward(change, -1, j))
-                if j == 0:
-                    summarize()
             own()
 
         gather_all(sum_f, 0).wait_recv()
@@ -248,15 +245,13 @@
             misfit = observed_ref[:, columns[j]].astype(jnp.float32) - (predicted + arrived[j])
             misfit_ref[:, columns[j]] = misfit
             misfit_wire[j] = misfit.astype(jnp.bfloat16)
-            for at, steps in ((NEXT, 1), (PARTNER, -1)):
+            for at, steps in ((NEXT, 1), (FAR, -2), (PARTNER, -1)):
                 halo(misfit_wire.at[j], misfit_in, 1, at, j, steps).start()
-        for j in range(chunks):
-            halo(misfit_wire.at[j], misfit_in, 1, FAR, j, -2).start()
 
         data = jnp.concatenate([misfit_wire[j] for j in range(chunks)], 1)
         sum_b[0] = pick(
             mm(basis(0), jnp.concatenate([data] * layers, 0), NT)
-        )
+        ).astype(jnp.bfloat16)
         gather_start(sum_b, 1, -1)
         for l in range(layers):
             for cols in columns:
@@ -277,14 +272,14 @@
         for j in range(chunks // 2, chunks):
             relay(j)
         backward(misfit_in.at[NEXT], tile_slot(1))
-        received(HANDED, -1)
-        backward(misfit_in.at[HANDED], tile_slot(-2))
+        received(FAR, -2)
+        backward(misfit_in.at[FAR], tile_slot(2))
         gather_all(sum_b, 1).wait_recv()
         near[...] += sum(
             mm(part, basis(1)) for part in spread(sum_b[...], 1)
         ).reshape(layers, perts, points)
-        received(FAR, -2)
-        backward(misfit_in.at[FAR], tile_slot(2))
+        received(HANDED, -1)
+        backward(misfit_in.at[HANDED], tile_slot(-2))
         model = model_ref[...]
         model_ref[...] = model + 0.01 * (near[...] - 10.0 * model)
         for j in range(chunks):
@@ -348,7 +343,7 @@
             pltpu.VMEM((chunks, perts, CHUNK), jnp.float32),
             pltpu.VMEM((layers, perts, points), jnp.float32),
             pltpu.VMEM((n, rank, layers * perts), jnp.float32),
-            pltpu.VMEM((n, rank, layers * perts), jnp.float32),
+            pltpu.VMEM((n, rank, layers * perts), jnp.bfloat16),
             pltpu.SemaphoreType.DMA((layers, span)),
             pltpu.SemaphoreType.DMA((5,)),
             pltpu.SemaphoreType.DMA((4, layers)),

time: 86.2 us -> 79.3 us (0.920)
  Pallas kernels: 83.2 us -> 75.7 us
    pallas_call x1, Pallas kernels: 83.2 us -> 75.7 us  [on_device(): pl.pallas_call(functools.partial(kernel, n), out_shape=(jax.ShapeDtypeStr...]
where the time goes in v4:
time: 79.3 us; the launch traced here: 78.5 us
  Pallas kernels  75.7 us (95%)
  local copies, waits for them, and re-layouts  2.15 us (3%)
    pallas_call x1, Pallas kernels, on_device(): pl.pallas_call(functools.partial(kernel, n), out_shape=(jax.ShapeDtypeStr...  75.7 us
    unnamed x4, local copies, waits for them, and re-layouts  2.15 us

profile of v4, /device:TPU:0, one launch (start us, length us, event | category | flops | bytes accessed | tf_op | source)
XLA Modules:
  0.0 78.5 jit_solution(5959333999853000116)
XLA Ops:
  0.6 0.0 copy-start
  0.6 0.6 copy-done
  1.3 75.7 %shard_map.86 = (f32[2,64,1024]{2,1,0:T(8,128)S(1)}, f32[64,1024]{1,0:T(8,128)S(1)}) custom-call(s32[5]{0:T(128)S(1)} %copy-done, bf16[2,5,1024,1024]{3,2,1,0:T(8,128)(2,1)} %tiles_hbm.1, bf16[2,16,1024]{2,1,0:T(8,128)(2,1)} %bitcast.2, bf16[2,16,1024]{2,1,0:T(8,128)(2,1)} %bitcast.3, f32[2,16,16,16]{3,2,1,0:T(8,128)} %coupling_hbm.1, ...), custom_call_target="tpu_custom_call" | custom-call | tf_op jit(solution)/shard_map/pallas_call | solution.py:316
  77.0 0.8 %copy.11 = f32[2,64,1024]{2,1,0:T(8,128)} copy(f32[2,64,1024]{2,1,0:T(8,128)S(1)} %get-tuple-element.4) | data formatting | bytes 1048576
  77.8 0.7 copy.12
Async XLA Ops:
  0.6 0.7 copy-start

commit v5 on v4

--- a/solution.py
+++ b/solution.py
@@ -9,7 +9,7 @@
 
 RADIUS = 2
 ITERS = 3
-CHUNK = 512
+CHUNK = 256
 HANDED, FAR, PARTNER, NEXT = range(4)
 NT = (((1,), (1,)), ((), ()))
 NN = (((1,), (0,)), ((), ()))

time: 79.3 us -> 88.4 us (1.11)
  Pallas kernels: 75.7 us -> 84.7 us
    pallas_call x1, Pallas kernels: 75.7 us -> 84.7 us  [on_device(): pl.pallas_call(functools.partial(kernel, n), out_shape=(jax.ShapeDtypeStr...]
where the time goes in v5:
time: 88.4 us; the launch traced here: 87.5 us
  Pallas kernels  84.7 us (96%)
  local copies, waits for them, and re-layouts  2.15 us (2%)
    pallas_call x1, Pallas kernels, on_device(): pl.pallas_call(functools.partial(kernel, n), out_shape=(jax.ShapeDtypeStr...  84.7 us
    unnamed x4, local copies, waits for them, and re-layouts  2.15 us

profile of v5, /device:TPU:0, one launch (start us, length us, event | category | flops | bytes accessed | tf_op | source)
XLA Modules:
  0.0 87.5 jit_solution(9444483976464781095)
XLA Ops:
  0.6 0.0 copy-start
  0.6 0.6 copy-done
  1.3 84.7 %shard_map.86 = (f32[2,64,1024]{2,1,0:T(8,128)S(1)}, f32[64,1024]{1,0:T(8,128)S(1)}) custom-call(s32[5]{0:T(128)S(1)} %copy-done, bf16[2,5,1024,1024]{3,2,1,0:T(8,128)(2,1)} %tiles_hbm.1, bf16[2,16,1024]{2,1,0:T(8,128)(2,1)} %bitcast.2, bf16[2,16,1024]{2,1,0:T(8,128)(2,1)} %bitcast.3, f32[2,16,16,16]{3,2,1,0:T(8,128)} %coupling_hbm.1, ...), custom_call_target="tpu_custom_call" | custom-call | tf_op jit(solution)/shard_map/pallas_call | solution.py:316
  86.0 0.8 copy.11
  86.8 0.7 copy.12
Async XLA Ops:
  0.6 0.7 copy-start
